TPU v7x, 32 devices: a whole 2x2x4 slice. The times are simulated.
32 devices in a mesh: dp: 4 (over y, x), fsdp: 4 (over z), tensor: 2 (over core).
Axes of the slice: x: 2, y: 2, z: 4, core: 2. Of those that a mesh axis runs over, the one named last changes fastest.
Arguments:
- tokens: bfloat16 [1024, 8192], P(('dp', 'tensor'), 'fsdp'), parts along dimension 0, may hold values from -6 to 6
- gate_weight: bfloat16 [8192, 14336], P('fsdp', 'tensor'), may hold values from -0.09375 to 0.09375
- up_weight: bfloat16 [8192, 14336], P('fsdp', 'tensor'), may hold values from -0.09375 to 0.09375
- down_weight: bfloat16 [14336, 8192], P('tensor', 'fsdp'), may hold values from -0.0625 to 0.0625
- gate_mask: int32 [128, 224], P('fsdp', 'tensor'), may hold values from 0 to 1, as said below
- up_mask: int32 [128, 224], P('fsdp', 'tensor'), may hold values from 0 to 1, as said below
- down_mask: int32 [224, 128], P('tensor', 'fsdp'), may hold values from 0 to 1, as said below
Outputs:
- mixed: bfloat16 [1024, 8192], P(('dp', 'tensor'), 'fsdp'), parts along dimension 0
There are 4 independent parts, one for each index of `dp`. A program takes and returns all parts, laid end to end along the dimension named above; an argument that names none is the same for every part. Nothing has to cross between parts.
Inputs may be any that keep to these rules, and one draw needn't show every extreme that they name: `gate_mask`: 1 keeps a tile, 0 prunes it; each tile column of the gate and up masks and each tile row of the down mask has its own share of kept tiles. `up_mask`: as gate_mask. `down_mask`: as gate_mask, by tile rows.
All inputs are finite; a program needn't handle non-finite values.
Results may differ from a plain program's by a relative error of at most 0.0051.
Values may be sent and summed in bfloat16 or wider, within the bound.
A program may use at most 448 MiB of HBM per device.

v0:
```python
import jax
import jax.numpy as jnp
from jax import lax
from jax.sharding import PartitionSpec as P

BLOCK = 64


def apply_mask(weight, mask):
    rows, cols = weight.shape
    tiles = weight.reshape(rows // BLOCK, BLOCK, cols // BLOCK, BLOCK)
    kept = tiles * mask[:, None, :, None].astype(weight.dtype)
    return kept.reshape(rows, cols)


def body(tokens, gate_weight, up_weight, down_weight, gate_mask, up_mask, down_mask):
    gate_pruned = apply_mask(gate_weight, gate_mask)
    up_pruned = apply_mask(up_weight, up_mask)
    down_pruned = apply_mask(down_weight, down_mask)
    gate_group, up_group = (
        lax.all_to_all(gate_pruned, "fsdp", split_axis=1, concat_axis=0, tiled=True),
        lax.all_to_all(up_pruned, "fsdp", split_axis=1, concat_axis=0, tiled=True),
    )
    width = gate_group.shape[1]
    both = jnp.concatenate([gate_group, up_group], axis=1)
    feature_block = lax.all_gather(tokens, "fsdp", axis=1, tiled=True)
    summed = jnp.dot(
        lax.all_gather(feature_block, "tensor", axis=0, tiled=True),
        both,
        preferred_element_type=jnp.float32,
    )
    hidden = (jax.nn.silu(summed[:, :width]) * summed[:, width:]).astype(jnp.bfloat16)
    hidden_all = lax.all_gather(hidden, "fsdp", axis=1, tiled=True)
    mixed = lax.psum_scatter(
        jnp.dot(hidden_all, down_pruned, preferred_element_type=jnp.float32),
        "tensor",
        scatter_dimension=0,
        tiled=True,
    )
    return mixed.astype(jnp.bfloat16)


def solution(mesh):
    placed = (
        P(("dp", "tensor"), "fsdp"),
        P("fsdp", "tensor"),
        P("fsdp", "tensor"),
        P("tensor", "fsdp"),
        P("fsdp", "tensor"),
        P("fsdp", "tensor"),
        P("tensor", "fsdp"),
    )
    return jax.shard_map(
        body, mesh=mesh, in_specs=placed, out_specs=P(("dp", "tensor"), "fsdp"), check_vma=False
    )
```

profile of v0, /device:TPU:0, one launch (start us, length us, event | category | flops | bytes accessed | tf_op | source)
XLA Modules:
  0.0 1631.2 jit_solution(6381841073487537280)
XLA Ops:
  6.5 0.7 convert_element_type.18
  7.3 18.9 %mul.40 = bf16[32,64,112,64]{3,2,1,0:T(8,128)(2,1)} broadcast(bf16[32,112]{1,0:T(8,128)(2,1)S(1)} %convert_element_type.18), dimensions={0,2} | broadcast | bytes 29367296 | tf_op jit(solution)/shard_map/mul | solution.py:12
  26.1 67.0 %mul.41 = bf16[2048,7168]{1,0:T(8,128)(2,1)} reshape(bf16[32,64,112,64]{3,2,1,0:T(8,128)(2,1)} %mul.40) | data formatting | bytes 58720256 | tf_op jit(solution)/shard_map/mul | solution.py:12
  93.1 29.7 %mul.42 = bf16[2048,7168]{1,0:T(8,128)(2,1)} multiply(bf16[2048,7168]{1,0:T(8,128)(2,1)} %param.8, bf16[2048,7168]{1,0:T(8,128)(2,1)} %mul.41) | non-fusion elementwise | flops 14680064 | bytes 88080384 | tf_op jit(solution)/shard_map/mul | solution.py:12
  122.8 20.3 %copy.17 = bf16[256,4,8,1792]{3,2,0,1:T(8,128)(2,1)} copy(bf16[256,4,8,1792]{3,2,1,0:T(8,128)(2,1)} %bitcast.26) | data formatting | bytes 58720256 | tf_op jit(solution)/shard_map/all_to_all | solution.py:21
  143.2 0.0 copy-start
  143.2 9.2 all-to-all-start
  152.4 0.0 copy-done
  152.4 19.0 %mul.43 = bf16[32,64,112,64]{3,2,1,0:T(8,128)(2,1)} broadcast(bf16[32,112]{1,0:T(8,128)(2,1)S(1)} %convert_element_type.19), dimensions={0,2} | broadcast | bytes 29367296 | tf_op jit(solution)/shard_map/mul | solution.py:12
  171.4 67.0 %mul.44 = bf16[2048,7168]{1,0:T(8,128)(2,1)} reshape(bf16[32,64,112,64]{3,2,1,0:T(8,128)(2,1)} %mul.43) | data formatting | bytes 58720256 | tf_op jit(solution)/shard_map/mul | solution.py:12
  238.4 29.7 %mul.45 = bf16[2048,7168]{1,0:T(8,128)(2,1)} multiply(bf16[2048,7168]{1,0:T(8,128)(2,1)} %param.9, bf16[2048,7168]{1,0:T(8,128)(2,1)} %mul.44) | non-fusion elementwise | flops 14680064 | bytes 88080384 | tf_op jit(solution)/shard_map/mul | solution.py:12
  268.1 20.3 %copy.16 = bf16[256,4,8,1792]{3,2,0,1:T(8,128)(2,1)} copy(bf16[256,4,8,1792]{3,2,1,0:T(8,128)(2,1)} %bitcast.27) | data formatting | bytes 58720256 | tf_op jit(solution)/shard_map/all_to_all | solution.py:22
  288.4 498.3 %all-to-all-done = bf16[2048,4,1792]{2,0,1:T(8,128)(2,1)} async-done(((bf16[2048,4,1792]{2,0,1:T(8,128)(2,1)}), bf16[2048,4,1792]{2,0,1:T(8,128)(2,1)}, u32[]{:S(2)}, u32[]{:S(2)}) %all-to-all-start) | async-done | bytes 29360160 | tf_op jit(solution)/shard_map/all_to_all | solution.py:21
  786.7 9.1 all-to-all-start.1
  795.8 0.0 all-gather.4.cloned.1.call-start
  795.8 0.7 all-gather.4.cloned.1.call-update
  796.5 0.0 all-gather.6.cloned.1.call-start
  796.6 211.5 %all-gather.4.cloned.1.call-done = bf16[128,8192]{1,0:T(8,128)(2,1)} async-done(((bf16[128,2048]{1,0:T(8,128)(2,1)}), bf16[128,8192]{1,0:T(8,128)(2,1)}) %all-gather.4.cloned.1.call-update) | async-done | bytes 2097168 | tf_op jit(solution)/shard_map/all_gather | solution.py:26
  1008.0 0.0 all-gather.6.cloned.1.call-update
  1008.0 0.0 all-gather.8.cloned.1.call-start
  1008.1 13.2 all-gather.6.cloned.1.call-done
  1021.3 440.4 %all-to-all-done.1 = bf16[2048,4,1792]{2,0,1:T(8,128)(2,1)} async-done(((bf16[2048,4,1792]{2,0,1:T(8,128)(2,1)}), bf16[2048,4,1792]{2,0,1:T(8,128)(2,1)}, u32[]{:S(2)}, u32[]{:S(2)}) %all-to-all-start.1) | async-done | bytes 29360160 | tf_op jit(solution)/shard_map/all_to_all | solution.py:22
  1461.7 0.0 copy-start.1
  1461.7 26.3 %fusion.6 = f32[256,3584]{0,1:T(8,128)} fusion(bf16[256,8192]{1,0:T(8,128)(2,1)} %all-gather.6.cloned.1.call-done, bf16[8192,1792]{1,0:T(8,128)(2,1)} %bitcast.3, bf16[8192,1792]{1,0:T(8,128)(2,1)} %bitcast.1), kind=kOutput, calls=%fused_computation.8 | convolution fusion | flops 15149826048 | bytes 66584576 | tf_op jit(solution)/shard_map/dot_general | solution.py:27
  1488.0 3.5 fusion.9
  1491.6 0.0 all-gather.8.cloned.1.call-update
  1491.6 0.2 reduce-scatter.2.cloned.1.call-start
  1491.8 0.0 copy-done.1
  1491.9 0.1 copy.11
  1492.0 19.3 %mul.48 = bf16[112,64,32,64]{3,2,1,0:T(8,128)(2,1)} broadcast(bf16[112,32]{1,0:T(8,128)(2,1)S(1)} %copy.11), dimensions={0,2} | broadcast | bytes 29367296 | tf_op jit(solution)/shard_map/mul | solution.py:12
  1511.3 79.2 %mul.49 = bf16[7168,2048]{1,0:T(8,128)(2,1)} reshape(bf16[112,64,32,64]{3,2,1,0:T(8,128)(2,1)} %mul.48) | data formatting | bytes 58720256 | tf_op jit(solution)/shard_map/mul | solution.py:12
  1590.5 0.0 all-gather.8.cloned.1.call-done
  1590.5 23.3 %fusion.4 = f32[256,2048]{1,0:T(8,128)} fusion(bf16[256,7168]{0,1:T(8,128)(2,1)} %all-gather.8.cloned.1.call-done, bf16[7168,2048]{1,0:T(8,128)(2,1)} %param.10, bf16[7168,2048]{1,0:T(8,128)(2,1)} %mul.49), kind=kOutput, calls=%fused_computation.6 | convolution fusion | flops 7530872832 | bytes 64487424 | tf_op jit(solution)/shard_map/dot_general | solution.py:35
  1613.8 0.0 reduce-scatter.2.cloned.1.call-update
  1613.9 8.7 reduce-scatter.2.cloned.1.call-done
  1622.5 2.1 convert_element_type.22
  (2 shorter events, 0.0 us)
Async XLA Ops:
  143.2 9.2 copy-start
  143.2 643.5 %all-to-all-start = ((bf16[2048,4,1792]{2,0,1:T(8,128)(2,1)}), bf16[2048,4,1792]{2,0,1:T(8,128)(2,1)}, u32[]{:S(2)}, u32[]{:S(2)}) async-start(bf16[2048,4,1792]{2,0,1:T(8,128)(2,1)} %bitcast.25), calls=%async_computation | async-start | bytes 58720256 | tf_op jit(solution)/shard_map/all_to_all | solution.py:21
  786.7 675.0 %all-to-all-start.1 = ((bf16[2048,4,1792]{2,0,1:T(8,128)(2,1)}), bf16[2048,4,1792]{2,0,1:T(8,128)(2,1)}, u32[]{:S(2)}, u32[]{:S(2)}) async-start(bf16[2048,4,1792]{2,0,1:T(8,128)(2,1)} %bitcast.24), calls=%async_computation.1 | async-start | bytes 58720256 | tf_op jit(solution)/shard_map/all_to_all | solution.py:22
  795.8 212.2 %all-gather.4.cloned.1.call-start = ((), (), s32[]{:S(2)}) async-start(), calls=%async_computation.3 | async-start | bytes 2621440 | tf_op jit(solution)/shard_map/all_gather | solution.py:26
  796.5 224.8 %all-gather.6.cloned.1.call-start = ((), (), s32[]{:S(2)}) async-start(), calls=%async_computation.4 | async-start | bytes 6291456 | tf_op jit(solution)/shard_map/all_gather | solution.py:28
  1008.0 582.5 %all-gather.8.cloned.1.call-start = ((), (), s32[]{:S(2)}) async-start(), calls=%async_computation.5 | async-start | bytes 4587520 | tf_op jit(solution)/shard_map/all_gather | solution.py:33
  1461.7 30.1 %copy-start.1 = (s32[112,32]{0,1:T(8,128)S(1)}, s32[112,32]{0,1:T(8,128)}, u32[]{:S(2)}) copy-start(s32[112,32]{0,1:T(8,128)} %param.13) | copy-start | bytes 43012
  1491.6 130.9 %reduce-scatter.2.cloned.1.call-start = ((), (), s32[]{:S(2)}) async-start(), calls=%async_computation.6 | async-start | bytes 3145728 | tf_op jit(solution)/shard_map/reduce_scatter | solution.py:34
Sparse Core Ops, SparseCore 0:
  798.2 209.7 all-gather.3
  1009.6 11.7 all-gather.5
  1491.7 71.0 all-gather.7
  1614.0 8.5 reduce-scatter.1
where the time goes:
time: 1640 us; the launch traced here: 1630 us
  waiting for transfers between devices  1170 us (71%)
  local copies, waits for them, and re-layouts  311 us (19%)
  other arithmetic  65.7 us (4%)
  matrix products  49.7 us (3%)
  starting transfers between devices  18.6 us (1%)
    all_to_all x1, waiting for transfers between devices, body(): lax.all_to_all(gate_pruned, 'fsdp', split_axis=1, concat_axis=0, tiled=True)  498 us
    all_to_all x1, waiting for transfers between devices, body(): lax.all_to_all(up_pruned, 'fsdp', split_axis=1, concat_axis=0, tiled=True)  440 us
    mul x6, local copies, waits for them, and re-layouts, apply_mask(): kept = tiles * mask[:, None, :, None].astype(weight.dtype)  270 us
    all_gather x1, waiting for transfers between devices, body(): feature_block = lax.all_gather(tokens, 'fsdp', axis=1, tiled=True)  211 us
    mul x2, other arithmetic, apply_mask(): kept = tiles * mask[:, None, :, None].astype(weight.dtype)  59.4 us
  transfers between devices with their start and end apart: 6, of which 5 were waited for; matrix products, arithmetic and copies ran while one was open for 14% of the time, Pallas kernels for 0%

commit v1 on v0

v1 whole, which is shorter than its diff:
```python
import functools

import jax
import jax.numpy as jnp
from jax import lax
from jax.experimental import pallas as pl
from jax.experimental.pallas import tpu as pltpu
from jax.sharding import PartitionSpec as P

BLOCK = 64
MESH = pl.DeviceIdType.MESH
DEPTH = 3
LAG_SUM = 2
LAG_HID = 2
F32 = jnp.float32
BF16 = jnp.bfloat16


def both(lo, value, hi):
    return jnp.logical_and(value >= lo, value < hi)


def kernel(F, T, n, NS, tokens, gate, up, down, gmask, umask, dmask, out,
           tok, wbuf, wm, part, slot, hid, dbuf, dm, dexp, acc, xbuf,
           tok_ssem, tok_rsem, wsem, dsem, rs_ssem, rs_rsem, ag_ssem, ag_rsem, x_ssem, x_rsem):
    z = lax.axis_index("fsdp")
    c = lax.axis_index("tensor")
    last = F - 1
    pos = (z, last - z)
    ahead = (z + 1, z - 1)
    back = (z - 1, z + 1)
    rows = tokens.shape[0]
    depth = gate.shape[0]
    width = down.shape[1]
    tiles = n // BLOCK

    def chunk(d, s):
        return d * NS + s

    def w_copies(d, s):
        b = lax.rem(s, DEPTH)
        cols = pl.ds(pl.multiple_of(chunk(d, s) * n, n), n)
        return (
            pltpu.make_async_copy(gate.at[:, cols], wbuf.at[d, b, :, 0:n], wsem.at[d, b, 0]),
            pltpu.make_async_copy(up.at[:, cols], wbuf.at[d, b, :, n:2 * n], wsem.at[d, b, 1]),
        )

    def d_copy(d, s):
        b = lax.rem(s, DEPTH)
        span = pl.ds(pl.multiple_of(chunk(d, s) * n, n), n)
        return pltpu.make_async_copy(down.at[span, :], dbuf.at[d, b], dsem.at[d, b])

    def rs_copy(d, s):
        return pltpu.make_async_remote_copy(
            src_ref=slot.at[d, s], dst_ref=slot.at[d, s],
            send_sem=rs_ssem.at[d, s], recv_sem=rs_rsem.at[d, s],
            device_id={"fsdp": ahead[d]}, device_id_type=MESH)

    def ag_copy(d, s):
        return pltpu.make_async_remote_copy(
            src_ref=hid.at[d, s], dst_ref=hid.at[d, s],
            send_sem=ag_ssem.at[d, s], recv_sem=ag_rsem.at[d, s],
            device_id={"fsdp": back[d]}, device_id_type=MESH)

    def row_block(i):
        return pl.ds(pl.multiple_of(i * rows, rows), rows)

    def tok_copy(j, owner):
        return pltpu.make_async_remote_copy(
            src_ref=tokens, dst_ref=tok.at[row_block(owner), :],
            send_sem=tok_ssem.at[j - 1], recv_sem=tok_rsem.at[j - 1],
            device_id={"tensor": lax.rem(c + j, T)}, device_id_type=MESH)

    def x_copy(j):
        partner = lax.rem(c + j, T)
        return pltpu.make_async_remote_copy(
            src_ref=acc.at[row_block(partner), :], dst_ref=xbuf.at[j - 1],
            send_sem=x_ssem.at[j - 1], recv_sem=x_rsem.at[j - 1],
            device_id={"tensor": partner}, device_id_type=MESH)

    for s in range(min(DEPTH - 1, NS)):
        for d in range(2):
            for copy in w_copies(d, s):
                copy.start()

    barrier = pltpu.get_barrier_semaphore()
    for j in range(1, T):
        pl.semaphore_signal(barrier, inc=1, device_id={"tensor": lax.rem(c + j, T)}, device_id_type=MESH)

    @pl.when(z > 0)
    def _():
        pl.semaphore_signal(barrier, inc=1, device_id={"fsdp": z - 1}, device_id_type=MESH)

    @pl.when(z < last)
    def _():
        pl.semaphore_signal(barrier, inc=1, device_id={"fsdp": z + 1}, device_id_type=MESH)

    inner = jnp.logical_and(z > 0, z < last)
    ends = 1 if F > 1 else 0

    @pl.when(inner)
    def _():
        pl.semaphore_wait(barrier, T - 1 + 2)

    @pl.when(jnp.logical_not(inner))
    def _():
        pl.semaphore_wait(barrier, T - 1 + ends)

    for j in range(1, T):
        tok_copy(j, c).start()
    for s in range(min(DEPTH - 1, NS)):
        for d in range(2):
            d_copy(d, s).start()
    tok[row_block(c), :] = tokens[...]
    acc[...] = jnp.zeros_like(acc)
    spread = (lax.broadcasted_iota(jnp.int32, (dmask.shape[1], width), 1) // BLOCK
              == lax.broadcasted_iota(jnp.int32, (dmask.shape[1], width), 0))
    dexp[...] = jnp.dot(dmask[...].astype(F32).astype(BF16), spread.astype(F32).astype(BF16),
                        preferred_element_type=F32)
    for j in range(1, T):
        tok_copy(j, lax.rem(c + T - j, T)).wait_recv()

    def first_product(d, s):
        b = lax.rem(s, DEPTH)
        for copy in w_copies(d, s):
            copy.wait()

        @pl.when(s + DEPTH - 1 < NS)
        def _():
            for copy in w_copies(d, s + DEPTH - 1):
                copy.start()

        hit = (lax.broadcasted_iota(jnp.int32, (gmask.shape[1], n), 1) // BLOCK + chunk(d, s) * tiles
               == lax.broadcasted_iota(jnp.int32, (gmask.shape[1], n), 0))
        hit = hit.astype(F32).astype(BF16)
        for k, mask in enumerate((gmask, umask)):
            kept = jnp.dot(mask[...].astype(F32).astype(BF16), hit, preferred_element_type=F32).astype(BF16)
            for r in range(depth // BLOCK):
                span = slice(r * BLOCK, (r + 1) * BLOCK)
                wm[span, k * n:(k + 1) * n] = wbuf[d, b, span, k * n:(k + 1) * n] * kept[r:r + 1, :]
        part[d] = jnp.dot(tok[...], wm[...], preferred_element_type=F32)

    def combine(d, s):
        @pl.when(pos[d] > 0)
        def _():
            rs_copy(d, s).wait_recv()

            @pl.when(pos[d] < last)
            def _():
                slot[d, s] = (part[d] + slot[d, s].astype(F32)).astype(BF16)

            @pl.when(pos[d] == last)
            def _():
                g = part[d, :, 0:n] + slot[d, s, :, 0:n].astype(F32)
                u = part[d, :, n:2 * n] + slot[d, s, :, n:2 * n].astype(F32)
                hid[d, s] = (g / (1.0 + jnp.exp(-g)) * u).astype(BF16)

        @pl.when(pos[d] == 0)
        def _():
            slot[d, s] = part[d].astype(BF16)

        @pl.when(pos[d] < last)
        def _():
            rs_copy(d, s).start()

    def pass_hidden(d, s):
        @pl.when(pos[d] < last)
        def _():
            ag_copy(d, s).wait_recv()

        @pl.when(pos[d] > 0)
        def _():
            ag_copy(d, s).start()

    def second_product(d, s):
        b = lax.rem(s, DEPTH)
        d_copy(d, s).wait()

        @pl.when(s + DEPTH - 1 < NS)
        def _():
            d_copy(d, s + DEPTH - 1).start()

        for i in range(tiles):
            span = slice(i * BLOCK, (i + 1) * BLOCK)
            kept = dexp[pl.ds(chunk(d, s) * tiles + i, 1), :].astype(BF16)
            dm[span, :] = dbuf[d, b, span, :] * kept
        step = min(512, width)
        for i in range(width // step):
            span = slice(i * step, (i + 1) * step)
            acc[:, span] += jnp.dot(hid[d, s], dm[:, span], preferred_element_type=F32)

    def body(t, carry):
        s_sum = [t - LAG_SUM * pos[d] for d in range(2)]
        s_hid = [t - LAG_SUM * last - LAG_HID * (last - pos[d]) for d in range(2)]
        for fn, at in ((first_product, s_sum), (combine, s_sum), (pass_hidden, s_hid), (second_product, s_hid)):
            for d in range(2):
                pl.when(both(0, at[d], NS))(functools.partial(fn, d, at[d]))
        return carry

    lax.fori_loop(0, NS + (LAG_SUM + LAG_HID) * last, body, 0)

    for j in range(1, T):
        x_copy(j).start()

    def drain(s, carry):
        for d in range(2):
            @pl.when(pos[d] < last)
            def _():
                rs_copy(d, s).wait_send()

            @pl.when(pos[d] > 0)
            def _():
                ag_copy(d, s).wait_send()
        return carry

    lax.fori_loop(0, NS, drain, 0)
    for j in range(1, T):
        tok_copy(j, c).wait_send()
        x_copy(j).wait_recv()
    total = acc[row_block(c), :]
    for j in range(1, T):
        total = total + xbuf[j - 1]
    out[...] = total.astype(BF16)
    for j in range(1, T):
        x_copy(j).wait_send()


def solution(mesh):
    F, T = mesh.shape["fsdp"], mesh.shape["tensor"]
    placed = (
        P(("dp", "tensor"), "fsdp"),
        P("fsdp", "tensor"),
        P("fsdp", "tensor"),
        P("tensor", "fsdp"),
        P("fsdp", "tensor"),
        P("fsdp", "tensor"),
        P("tensor", "fsdp"),
    )

    def body(tokens, gate, up, down, gmask, umask, dmask):
        rows, depth = tokens.shape
        units, width = down.shape
        n = 128
        NS = units // (2 * n)
        TT = rows * T
        vm = pltpu.VMEM
        dma = pltpu.SemaphoreType.DMA
        in_vmem = pl.BlockSpec(memory_space=pltpu.VMEM)
        in_hbm = pl.BlockSpec(memory_space=pl.ANY)
        return pl.pallas_call(
            functools.partial(kernel, F, T, n, NS),
            out_shape=jax.ShapeDtypeStruct((rows, width), BF16),
            in_specs=[in_vmem, in_hbm, in_hbm, in_hbm, in_vmem, in_vmem, in_vmem],
            out_specs=in_vmem,
            scratch_shapes=[
                vm((TT, depth), BF16),
                vm((2, DEPTH, depth, 2 * n), BF16),
                vm((depth, 2 * n), BF16),
                vm((2, TT, 2 * n), F32),
                vm((2, NS, TT, 2 * n), BF16),
                vm((2, NS, TT, n), BF16),
                vm((2, DEPTH, n, width), BF16),
                vm((n, width), BF16),
                vm((dmask.shape[0], width), F32),
                vm((TT, width), F32),
                vm((T - 1, rows, width), F32),
                dma((T - 1,)),
                dma((T - 1,)),
                dma((2, DEPTH, 2)),
                dma((2, DEPTH)),
                dma((2, NS)),
                dma((2, NS)),
                dma((2, NS)),
                dma((2, NS)),
                dma((T - 1,)),
                dma((T - 1,)),
            ],
            compiler_params=pltpu.CompilerParams(
                collective_id=0, has_side_effects=True, vmem_limit_bytes=56 * 1024 * 1024),
            cost_estimate=pl.CostEstimate(
                flops=6 * TT * depth * units, bytes_accessed=6 * depth * units, transcendentals=TT * units),
        )(tokens, gate, up, down, gmask, umask, dmask)

    return jax.shard_map(
        body, mesh=mesh, in_specs=placed, out_specs=P(("dp", "tensor"), "fsdp"), check_vma=False
    )
```

time: 1640 us -> 149 us (0.09)
  waiting for transfers between devices: 1170 us -> 0 us
  local copies, waits for them, and re-layouts: 311 us -> 3.32 us
  Pallas kernels: 0 us -> 146 us
  other arithmetic: 65.7 us -> 0 us
  matrix products: 49.7 us -> 0 us
  starting transfers between devices: 18.6 us -> 0 us
    all_to_all x2 -> x0, waiting for transfers between devices: 939 us -> none  [the longest x1 498 us: body(): lax.all_to_all(gate_pruned, 'fsdp', split_axis=1, concat_axis=0, tiled=True)]
    mul x6 -> x0, local copies, waits for them, and re-layouts: 270 us -> none  [apply_mask(): kept = tiles * mask[:, None, :, None].astype(weight.dtype)]
    all_gather x3 -> x0, waiting for transfers between devices: 225 us -> none  [the longest x1 211 us: body(): feature_block = lax.all_gather(tokens, 'fsdp', axis=1, tiled=True)]
    pallas_call x0 -> x1, Pallas kernels: none -> 146 us  [body(): pl.pallas_call(functools.partial(kernel, F, T, n, NS), out_shape=jax.Shap...]
    mul x2 -> x0, other arithmetic: 59.4 us -> none  [apply_mask(): kept = tiles * mask[:, None, :, None].astype(weight.dtype)]
    dot_general x2 -> x0, matrix products: 49.7 us -> none  [the longest x1 26.3 us: body(): jnp.dot(lax.all_gather(feature_block, 'tensor', axis=0, tiled=True), both...]
    all_to_all x2 -> x0, local copies, waits for them, and re-layouts: 40.7 us -> none  [the longest x1 20.3 us: body(): lax.all_to_all(gate_pruned, 'fsdp', split_axis=1, concat_axis=0, tiled=True)]
    all_to_all x2 -> x0, starting transfers between devices: 18.3 us -> none  [the longest x1 9.2 us: body(): lax.all_to_all(gate_pruned, 'fsdp', split_axis=1, concat_axis=0, tiled=True)]
  transfers between devices with their start and end apart: 6 -> 0, of which waited for: 5 -> 0; matrix products, arithmetic and copies ran while one was open for 14% -> 0% of each run, Pallas kernels for 0% -> 0%
where the time goes in v1:
time: 149 us
  Pallas kernels  146 us (98%)
  local copies, waits for them, and re-layouts  3.32 us (2%)
    pallas_call x1, Pallas kernels, body(): pl.pallas_call(functools.partial(kernel, F, T, n, NS), out_shape=jax.Shap...  146 us
    unnamed x2, local copies, waits for them, and re-layouts  3.32 us

profile of v1, /device:TPU:0, one launch (start us, length us, event | category | flops | bytes accessed | tf_op | source)
XLA Modules:
  0.0 149.2 jit_solution(5158660217095314485)
XLA Ops:
  0.0 1.4 copy.8.dmask
  1.4 145.8 %shard_map.73 = bf16[128,2048]{1,0:T(8,128)(2,1)} custom-call(bf16[128,2048]{1,0:T(8,128)(2,1)} %tokens.1, bf16[2048,7168]{1,0:T(8,128)(2,1)} %gate.1, bf16[2048,7168]{1,0:T(8,128)(2,1)} %up.1, bf16[7168,2048]{1,0:T(8,128)(2,1)} %down.1, s32[32,112]{1,0:T(8,128)} %gmask.1, s32[32,112]{1,0:T(8,128)} %umask.1, s32[112,32]{1,0:T(8,128)} %copy.8.dmask), custom_call_target="tpu_custom_call" | custom-call | flops 22548578304 | bytes 88080384 | tf_op jit(solution)/shard_map/pallas_call | solution.py:250
  147.3 1.9 %copy.10 = bf16[128,2048]{1,0:T(8,128)(2,1)} copy(bf16[128,2048]{1,0:T(8,128)(2,1)} %shard_map.73) | data formatting | bytes 1048576
